TPU v7x, 32 devices: a whole 2x2x4 slice. The times are simulated.
32 devices in a mesh: member: 4 (over y, x), space: 8 (over z, core).
Axes of the slice: x: 2, y: 2, z: 4, core: 2. Of those that a mesh axis runs over, the one named last changes fastest.
Arguments:
- prior_samples: float32 [256, 64, 2048], P('member', 'space'), may hold values from -6 to 6
- external_drive: float32 [64, 2048], P('space'), may hold values from -6 to 6
- obs_value: float32 [8, 16, 1024], P('space', 'member'), may hold values from -6 to 6
- obs_index: int32 [8, 16, 1024], P('space', 'member'), may hold values from 0 to 1023
- obs_weight: bfloat16 [8, 16, 1024], P('space', 'member'), may hold values from 0.5 to 8
Outputs:
- analysis: float32 [256, 64, 2048], P('member', 'space')
Inputs may be any that keep to these rules, and one draw needn't show every extreme that they name: `obs_index`: the cell is numbered row by row within the region: row times 128 plus column.
All inputs are finite; a program needn't handle non-finite values.
Results may differ from a plain program's by a relative error of at most 0.0017.
Values may be sent and summed in bfloat16 or wider, within the bound.
A program may use at most 128 MiB of HBM per device.

v0:
```python
import jax
import jax.numpy as jnp
from jax import lax
from jax.sharding import PartitionSpec as P

STEPS = 8
ITERS = 6


step_size = 0.1
vertical_diffusion = 4.0
lateral_diffusion = 0.5
damping = 0.5


def padded(cells, sides, width):
    for axis, dim in sides:
        count = lax.axis_size(axis)
        ends = count - 1
        head = lax.slice_in_dim(cells, 0, width, axis=dim)
        tail = lax.slice_in_dim(cells, cells.shape[dim] - width, cells.shape[dim], axis=dim)
        cells = jnp.concatenate(
            [
                lax.ppermute(tail, axis, [(i, (i + 1) % count) for i in range(ends)]),
                cells,
                lax.ppermute(head, axis, [((i + 1) % count, i) for i in range(ends)]),
            ],
            axis=dim,
        )
    return cells


def shifted(value, axis, steps):
    count = lax.axis_size(axis)
    first, last = (max(0, -steps), min(count, count - steps))
    return lax.ppermute(value, axis, [(source, source + steps) for source in range(first, last)])


def advance(extended, forcing_rows):
    current = extended[:, 1:-1]
    upper_rows = extended[:, :-2]
    lower_rows = extended[:, 2:]
    right_cells = jnp.roll(current, -1, axis=2)
    left_cells = jnp.roll(current, 1, axis=2)
    laplace = vertical_diffusion * (upper_rows + lower_rows - 2.0 * current) + lateral_diffusion * (
        right_cells + left_cells - 2.0 * current
    )
    advect = current * (right_cells - left_cells + (lower_rows - upper_rows)) * 0.5
    return current + step_size * (laplace - advect - damping * current + forcing_rows)


def taper_above(row_pos, row_span):
    distance = row_span - row_pos
    return jnp.exp(-2.0 * distance * distance / (row_span * row_span))


def taper_below(row_pos, row_span):
    distance = row_pos + 1.0
    return jnp.exp(-2.0 * distance * distance / (row_span * row_span))


def curvature_term(anomaly_obs, weights, innovation):
    scaled = (anomaly_obs.astype(jnp.float32) * weights[:, None, :]).astype(jnp.bfloat16)
    matrix = jnp.einsum("rko,rjo->rkj", scaled, anomaly_obs, preferred_element_type=jnp.float32)
    vector = jnp.einsum(
        "rko,ro->rk",
        anomaly_obs.astype(jnp.float32),
        weights * innovation.astype(jnp.float32),
        precision=lax.Precision.HIGHEST,
    )
    return (matrix, vector)


def local(prior_samples, external_drive, obs_value, obs_index, obs_weight):
    highest = lax.Precision.HIGHEST
    local_members, height, width_cols = prior_samples.shape
    member_groups = lax.axis_size("member")
    members_all = local_members * member_groups
    number_tiles = obs_index.shape[1]
    region_cols = width_cols // (member_groups * number_tiles)
    state_now = prior_samples
    for step_index in range(STEPS):
        extended = padded(state_now, (("space", 1),), 1)
        state_now = advance(extended, external_drive)
    split_state = state_now.reshape(
        local_members, height, member_groups, number_tiles, region_cols
    ).transpose(2, 3, 0, 1, 4)
    received = lax.all_to_all(split_state, "member", split_axis=0, concat_axis=2, tiled=True)
    states = received.reshape(number_tiles, members_all, height * region_cols)
    cell_index = obs_index[0]
    picked = jnp.take_along_axis(states, cell_index[:, None, :], axis=2)
    obs_mean = jnp.mean(picked, axis=1)
    anomaly_obs = (picked - obs_mean[:, None, :]).astype(jnp.bfloat16)
    innovation = lax.optimization_barrier((obs_value[0] - obs_mean).astype(jnp.bfloat16))
    own_weight = obs_weight[0].astype(jnp.float32)
    row_pos = (cell_index // region_cols).astype(jnp.float32)
    row_span = float(height)
    matrix_own, vector_own = curvature_term(anomaly_obs, own_weight, innovation)
    below_matrix, below_vector = curvature_term(
        anomaly_obs, own_weight * taper_above(row_pos, row_span), innovation
    )
    above_matrix, above_vector = curvature_term(
        anomaly_obs, own_weight * taper_below(row_pos, row_span), innovation
    )
    matrix_above, vector_above = (
        shifted(below_matrix.astype(jnp.bfloat16), "space", 1).astype(below_matrix.dtype),
        shifted(below_vector.astype(jnp.bfloat16), "space", 1).astype(below_vector.dtype),
    )
    matrix_below, vector_below = (
        shifted(above_matrix.astype(jnp.bfloat16), "space", -1).astype(above_matrix.dtype),
        shifted(above_vector.astype(jnp.bfloat16), "space", -1).astype(above_vector.dtype),
    )
    identity_k = jnp.eye(members_all, dtype=jnp.float32)
    curvature = (members_all - 1.0) * identity_k + matrix_above + matrix_own + matrix_below
    right_side = vector_above + vector_own + vector_below
    frobenius = jnp.sqrt(jnp.sum(curvature * curvature, axis=(1, 2)))
    iterate = curvature / frobenius[:, None, None]
    inverse = jnp.broadcast_to(identity_k, curvature.shape)
    for sweep_index in range(ITERS):
        middle = 1.5 * identity_k - 0.5 * jnp.einsum(
            "rij,rjk->rik", inverse, iterate, precision=highest
        )
        iterate = jnp.einsum("rij,rjk->rik", iterate, middle, precision=highest)
        inverse = jnp.einsum("rij,rjk->rik", middle, inverse, precision=highest)
    spread = inverse * (jnp.sqrt(members_all - 1.0) / jnp.sqrt(frobenius))[:, None, None]
    inner_step = jnp.einsum("rij,rj->ri", inverse, right_side, precision=highest)
    mean_shift = (
        jnp.einsum("rij,rj->ri", inverse, inner_step, precision=highest) / frobenius[:, None]
    )
    transform = spread + mean_shift[:, :, None]
    centre = jnp.mean(states, axis=1, keepdims=True)
    anomalies = states - centre
    analysed = centre + jnp.einsum("rkj,rkc->rjc", transform, anomalies, precision=highest)
    outgoing = analysed.reshape(1, number_tiles, member_groups, local_members, height, region_cols)
    returned = lax.all_to_all(outgoing, "member", split_axis=2, concat_axis=0, tiled=True)
    return (
        returned.reshape(member_groups, number_tiles, local_members, height, region_cols)
        .transpose(2, 3, 0, 1, 4)
        .reshape(local_members, height, width_cols)
    )


def solution(mesh):
    return jax.shard_map(
        local,
        mesh=mesh,
        in_specs=(
            P("member", "space", None),
            P("space", None),
            P("space", "member", None),
            P("space", "member", None),
            P("space", "member", None),
        ),
        out_specs=P("member", "space", None),
        check_vma=False,
    )
```

profile of v0, /device:TPU:9, one launch (start us, length us, event | category | flops | bytes accessed | tf_op | source)
XLA Modules:
  0.0 414.2 jit_solution(625828098819100295)
XLA Ops:
  0.0 4.6 %copy.40 = f32[64,8,2048]{2,0,1:T(8,128)S(1)} copy(f32[64,8,2048]{2,1,0:T(8,128)} %param.5) | data formatting | bytes 8388608 | tf_op args[0]
  14.6 4.4 %collective-permute-done.1 = f32[64,1,2048]{2,0,1:T(8,128)S(1)} collective-permute-done((f32[64,1,2048]{2,0,1:T(8,128)S(1)}, f32[64,1,2048]{2,0,1:T(8,128)S(1)}, u32[]{:S(2)}, u32[]{:S(2)}) %collective-permute-start.1) | collective-permute-done | bytes 524320 | tf_op jit(solution)/shard_map/ppermute | solution.py:26
  19.0 4.4 %multiply_add_fusion.7 = f32[64,8,2048]{2,0,1:T(8,128)S(1)} fusion(f32[64,8,2048]{2,0,1:T(8,128)S(1)} %copy.40, f32[64,8,2047]{2,0,1:T(8,128)S(1)} %get-tuple-element.54, f32[64,8,1]{2,0,1:T(8,128)S(1)} %get-tuple-element.56, f32[64,8,1]{2,0,1:T(8,128)S(1)} %get-tuple-element.55, f32[64,8,2047]{2,0,1:T(8,128)S(1)} %get-tuple-element.53, ...), kind=kLoop, calls=%fused_computation.52 | loop fusion | flops 24117248 | bytes 17891328 | tf_op jit(solution)/shard_map/add | solution.py:49
  31.7 4.4 %collective-permute-done.3 = f32[64,1,2048]{2,0,1:T(8,128)S(1)} collective-permute-done((f32[64,1,2048]{2,0,1:T(8,128)S(1)}, f32[64,1,2048]{2,0,1:T(8,128)S(1)}, u32[]{:S(2)}, u32[]{:S(2)}) %collective-permute-start.3) | collective-permute-done | bytes 524320 | tf_op jit(solution)/shard_map/ppermute | solution.py:26
  36.1 4.4 %multiply_add_fusion.6 = f32[64,8,2048]{2,0,1:T(8,128)S(1)} fusion(f32[64,8,2048]{2,0,1:T(8,128)S(1)} %multiply_add_fusion.7, f32[64,8,2047]{2,0,1:T(8,128)S(1)} %get-tuple-element.48, f32[64,8,1]{2,0,1:T(8,128)S(1)} %get-tuple-element.50, f32[64,8,1]{2,0,1:T(8,128)S(1)} %get-tuple-element.49, f32[64,8,2047]{2,0,1:T(8,128)S(1)} %get-tuple-element.47, ...), kind=kLoop, calls=%fused_computation.51 | loop fusion | flops 24117248 | bytes 17891328 | tf_op jit(solution)/shard_map/add | solution.py:49
  53.2 4.4 %multiply_add_fusion.5 = f32[64,8,2048]{2,0,1:T(8,128)S(1)} fusion(f32[64,8,2048]{2,0,1:T(8,128)S(1)} %multiply_add_fusion.6, f32[64,8,2047]{2,0,1:T(8,128)S(1)} %get-tuple-element.42, f32[64,8,1]{2,0,1:T(8,128)S(1)} %get-tuple-element.44, f32[64,8,1]{2,0,1:T(8,128)S(1)} %get-tuple-element.43, f32[64,8,2047]{2,0,1:T(8,128)S(1)} %get-tuple-element.41, ...), kind=kLoop, calls=%fused_computation.50 | loop fusion | flops 24117248 | bytes 17891328 | tf_op jit(solution)/shard_map/add | solution.py:49
  70.2 4.4 %multiply_add_fusion.4 = f32[64,8,2048]{2,0,1:T(8,128)S(1)} fusion(f32[64,8,2048]{2,0,1:T(8,128)S(1)} %multiply_add_fusion.5, f32[64,8,2047]{2,0,1:T(8,128)S(1)} %get-tuple-element.36, f32[64,8,1]{2,0,1:T(8,128)S(1)} %get-tuple-element.38, f32[64,8,1]{2,0,1:T(8,128)S(1)} %get-tuple-element.37, f32[64,8,2047]{2,0,1:T(8,128)S(1)} %get-tuple-element.35, ...), kind=kLoop, calls=%fused_computation.49 | loop fusion | flops 24117248 | bytes 17891328 | tf_op jit(solution)/shard_map/add | solution.py:49
  82.9 4.4 %collective-permute-done.9 = f32[64,1,2048]{2,0,1:T(8,128)S(1)} collective-permute-done((f32[64,1,2048]{2,0,1:T(8,128)S(1)}, f32[64,1,2048]{2,0,1:T(8,128)S(1)}, u32[]{:S(2)}, u32[]{:S(2)}) %collective-permute-start.9) | collective-permute-done | bytes 524320 | tf_op jit(solution)/shard_map/ppermute | solution.py:26
  87.3 4.4 %multiply_add_fusion.3 = f32[64,8,2048]{2,0,1:T(8,128)S(1)} fusion(f32[64,8,2048]{2,0,1:T(8,128)S(1)} %multiply_add_fusion.4, f32[64,8,2047]{2,0,1:T(8,128)S(1)} %get-tuple-element.30, f32[64,8,1]{2,0,1:T(8,128)S(1)} %get-tuple-element.32, f32[64,8,1]{2,0,1:T(8,128)S(1)} %get-tuple-element.31, f32[64,8,2047]{2,0,1:T(8,128)S(1)} %get-tuple-element.29, ...), kind=kLoop, calls=%fused_computation.48 | loop fusion | flops 24117248 | bytes 17891328 | tf_op jit(solution)/shard_map/add | solution.py:49
  104.4 4.4 %multiply_add_fusion.2 = f32[64,8,2048]{2,0,1:T(8,128)S(1)} fusion(f32[64,8,2048]{2,0,1:T(8,128)S(1)} %multiply_add_fusion.3, f32[64,8,2047]{2,0,1:T(8,128)S(1)} %get-tuple-element.24, f32[64,8,1]{2,0,1:T(8,128)S(1)} %get-tuple-element.26, f32[64,8,1]{2,0,1:T(8,128)S(1)} %get-tuple-element.25, f32[64,8,2047]{2,0,1:T(8,128)S(1)} %get-tuple-element.23, ...), kind=kLoop, calls=%fused_computation.47 | loop fusion | flops 24117248 | bytes 17891328 | tf_op jit(solution)/shard_map/add | solution.py:49
  121.5 4.4 %multiply_add_fusion.1 = f32[64,8,2048]{2,0,1:T(8,128)S(1)} fusion(f32[64,8,2048]{2,0,1:T(8,128)S(1)} %multiply_add_fusion.2, f32[64,8,2047]{2,0,1:T(8,128)S(1)} %get-tuple-element.18, f32[64,8,1]{2,0,1:T(8,128)S(1)} %get-tuple-element.20, f32[64,8,1]{2,0,1:T(8,128)S(1)} %get-tuple-element.19, f32[64,8,2047]{2,0,1:T(8,128)S(1)} %get-tuple-element.17, ...), kind=kLoop, calls=%fused_computation.46 | loop fusion | flops 24117248 | bytes 17891328 | tf_op jit(solution)/shard_map/add | solution.py:49
  128.1 12.5 %collective-permute-start.15 = (f32[64,1,2048]{2,0,1:T(8,128)S(1)}, f32[64,1,2048]{2,0,1:T(8,128)S(1)}, u32[]{:S(2)}, u32[]{:S(2)}) collective-permute-start(f32[64,1,2048]{2,0,1:T(8,128)S(1)} %get-tuple-element.9), channel_id=1, source_target_pairs={{1,0},{2,1},{3,2},{4,3},{5,4},{6,5},{7,6},{9,8},{10,9},{11,10},{12... | collective-permute-start | bytes 1572872 | tf_op jit(solution)/shard_map/ppermute | solution.py:26
  142.3 4.5 %multiply_add_fusion = f32[64,8,2048]{2,0,1:T(8,128)} fusion(f32[64,8,2048]{2,0,1:T(8,128)S(1)} %multiply_add_fusion.1, f32[64,8,2047]{2,0,1:T(8,128)S(1)} %get-tuple-element.12, f32[64,8,1]{2,0,1:T(8,128)S(1)} %get-tuple-element.14, f32[64,8,1]{2,0,1:T(8,128)S(1)} %get-tuple-element.13, f32[64,8,2047]{2,0,1:T(8,128)S(1)} %get-tuple-element.11, ...), kind=kLoop, calls=%fused_computation.45 | loop fusion | flops 24117248 | bytes 17891328 | tf_op jit(solution)/shard_map/add | solution.py:49
  146.9 6.0 %reshape.183 = f32[64,8,4,4,128]{4,3,2,0,1:T(4,128)} reshape(f32[64,8,2048]{2,0,1:T(8,128)} %multiply_add_fusion) | data formatting | bytes 8388608 | tf_op jit(solution)/shard_map/reshape | solution.py:85
  152.9 6.6 %copy.80 = f32[64,8,4,4,128]{4,1,0,3,2:T(8,128)} copy(f32[64,8,4,4,128]{4,3,2,0,1:T(4,128)} %reshape.183) | data formatting | bytes 8388608 | tf_op jit(solution)/shard_map/reshape | solution.py:85
  159.5 5.0 %all-to-all-start = ((f32[4,4,64,8,128]{4,3,2,1,0:T(8,128)}), f32[4,4,64,8,128]{4,3,2,1,0:T(8,128)}, u32[]{:S(2)}, u32[]{:S(2)}) async-start(f32[4,4,64,8,128]{4,3,2,1,0:T(8,128)} %bitcast.148), calls=%async_computation | async-start | bytes 8388608 | tf_op jit(solution)/shard_map/all_to_all | solution.py:88
  164.7 47.3 %all-to-all-done = f32[4,4,64,8,128]{4,3,2,1,0:T(8,128)} async-done(((f32[4,4,64,8,128]{4,3,2,1,0:T(8,128)}), f32[4,4,64,8,128]{4,3,2,1,0:T(8,128)}, u32[]{:S(2)}, u32[]{:S(2)}) %all-to-all-start) | async-done | bytes 4194336 | tf_op jit(solution)/shard_map/all_to_all | solution.py:88
  212.0 4.6 %copy.42 = f32[1,4,4,64,8,128]{5,4,3,2,1,0:T(8,128)} copy(f32[1,4,4,64,8,128]{5,4,3,1,2,0:T(8,128)} %bitcast.2) | data formatting | bytes 8388608 | tf_op jit(solution)/shard_map/all_to_all | solution.py:88
  216.6 5.0 %reshape.184 = f32[4,256,1024]{2,1,0:T(8,128)} reshape(f32[1,4,4,64,8,128]{5,4,3,2,1,0:T(8,128)} %copy.42) | data formatting | bytes 8388608 | tf_op jit(solution)/shard_map/reshape | solution.py:89
  221.6 5.4 %copy.43 = f32[4,256,1024]{1,2,0:T(8,128)} copy(f32[4,256,1024]{2,1,0:T(8,128)} %reshape.184) | data formatting | bytes 8388608 | tf_op jit(solution)/shard_map/reshape | solution.py:89
  227.0 69.1 %gather_fusion = f32[4096,256]{1,0:T(8,128)} fusion(f32[4,256,1024]{1,2,0:T(8,128)} %copy.43, s32[4096]{0:T(1024)S(1)} %bitcast.146), kind=kCustom, calls=%fused_computation | custom fusion | bytes 8421376 | tf_op jit(solution)/shard_map/jit(take_along_axis)/gather | solution.py:91
  296.1 5.3 %copy.44 = f32[4,1024,256]{1,2,0:T(8,128)} copy(f32[4,1024,256]{2,1,0:T(8,128)} %bitcast.147) | data formatting | bytes 8388608 | tf_op jit(solution)/shard_map/jit(take_along_axis)/gather | solution.py:91
  327.2 5.2 %collective-permute-done.17 = bf16[4,256,256]{2,1,0:T(8,128)(2,1)S(1)} collective-permute-done((bf16[4,256,256]{2,1,0:T(8,128)(2,1)S(1)}, bf16[4,256,256]{2,1,0:T(8,128)(2,1)S(1)}, u32[]{:S(2)}, u32[]{:S(2)}) %collective-permute-start.17) | collective-permute-done | bytes 524320 | tf_op jit(solution)/shard_map/ppermute | solution.py:36
  361.6 49.8 %all_to_all.30 = f32[1,4,4,64,8,128]{5,4,3,1,0,2:T(8,128)S(1)} all-to-all(f32[1,4,4,64,8,128]{5,4,3,1,0,2:T(8,128)S(1)} %copy.46), channel_id=1, replica_groups=mesh['member'=4,'space'=8] {'member'}, dimensions={2} | all-to-all | bytes 8388608 | tf_op jit(solution)/shard_map/all_to_all | solution.py:135
  (119 shorter events, 138.3 us)
Async XLA Ops:
  4.7 9.9 %collective-permute-start = (f32[64,1,2048]{2,0,1:T(8,128)S(1)}, f32[64,1,2048]{2,0,1:T(8,128)S(1)}, u32[]{:S(2)}, u32[]{:S(2)}) collective-permute-start(f32[64,1,2048]{2,0,1:T(8,128)S(1)} %get-tuple-element.52), channel_id=1, source_target_pairs={{0,1},{1,2},{2,3},{3,4},{4,5},{5,6},{6,7},{8,9},{9,10},{10,11},{11... | collective-permute-start | bytes 1572872 | tf_op jit(solution)/shard_map/ppermute | solution.py:24
  8.5 10.5 %collective-permute-start.1 = (f32[64,1,2048]{2,0,1:T(8,128)S(1)}, f32[64,1,2048]{2,0,1:T(8,128)S(1)}, u32[]{:S(2)}, u32[]{:S(2)}) collective-permute-start(f32[64,1,2048]{2,0,1:T(8,128)S(1)} %get-tuple-element.51), channel_id=1, source_target_pairs={{1,0},{2,1},{3,2},{4,3},{5,4},{6,5},{7,6},{9,8},{10,9},{11,10},{12... | collective-permute-start | bytes 1572872 | tf_op jit(solution)/shard_map/ppermute | solution.py:26
  10.6 8.4 %copy-start.2 = (f32[8,2048]{1,0:T(8,128)S(1)}, f32[8,2048]{1,0:T(8,128)}, u32[]{:S(2)}) copy-start(f32[8,2048]{1,0:T(8,128)} %param.6) | copy-start | bytes 196612
  23.6 8.0 %collective-permute-start.2 = (f32[64,1,2048]{2,0,1:T(8,128)S(1)}, f32[64,1,2048]{2,0,1:T(8,128)S(1)}, u32[]{:S(2)}, u32[]{:S(2)}) collective-permute-start(f32[64,1,2048]{2,0,1:T(8,128)S(1)} %get-tuple-element.46), channel_id=1, source_target_pairs={{0,1},{1,2},{2,3},{3,4},{4,5},{5,6},{6,7},{8,9},{9,10},{10,11},{11... | collective-permute-start | bytes 1572872 | tf_op jit(solution)/shard_map/ppermute | solution.py:24
  25.6 10.5 %collective-permute-start.3 = (f32[64,1,2048]{2,0,1:T(8,128)S(1)}, f32[64,1,2048]{2,0,1:T(8,128)S(1)}, u32[]{:S(2)}, u32[]{:S(2)}) collective-permute-start(f32[64,1,2048]{2,0,1:T(8,128)S(1)} %get-tuple-element.45), channel_id=1, source_target_pairs={{1,0},{2,1},{3,2},{4,3},{5,4},{6,5},{7,6},{9,8},{10,9},{11,10},{12... | collective-permute-start | bytes 1572872 | tf_op jit(solution)/shard_map/ppermute | solution.py:26
  40.7 8.0 %collective-permute-start.4 = (f32[64,1,2048]{2,0,1:T(8,128)S(1)}, f32[64,1,2048]{2,0,1:T(8,128)S(1)}, u32[]{:S(2)}, u32[]{:S(2)}) collective-permute-start(f32[64,1,2048]{2,0,1:T(8,128)S(1)} %get-tuple-element.40), channel_id=1, source_target_pairs={{0,1},{1,2},{2,3},{3,4},{4,5},{5,6},{6,7},{8,9},{9,10},{10,11},{11... | collective-permute-start | bytes 1572872 | tf_op jit(solution)/shard_map/ppermute | solution.py:24
  42.7 10.5 %collective-permute-start.5 = (f32[64,1,2048]{2,0,1:T(8,128)S(1)}, f32[64,1,2048]{2,0,1:T(8,128)S(1)}, u32[]{:S(2)}, u32[]{:S(2)}) collective-permute-start(f32[64,1,2048]{2,0,1:T(8,128)S(1)} %get-tuple-element.39), channel_id=1, source_target_pairs={{1,0},{2,1},{3,2},{4,3},{5,4},{6,5},{7,6},{9,8},{10,9},{11,10},{12... | collective-permute-start | bytes 1572872 | tf_op jit(solution)/shard_map/ppermute | solution.py:26
  57.8 8.0 %collective-permute-start.6 = (f32[64,1,2048]{2,0,1:T(8,128)S(1)}, f32[64,1,2048]{2,0,1:T(8,128)S(1)}, u32[]{:S(2)}, u32[]{:S(2)}) collective-permute-start(f32[64,1,2048]{2,0,1:T(8,128)S(1)} %get-tuple-element.34), channel_id=1, source_target_pairs={{0,1},{1,2},{2,3},{3,4},{4,5},{5,6},{6,7},{8,9},{9,10},{10,11},{11... | collective-permute-start | bytes 1572872 | tf_op jit(solution)/shard_map/ppermute | solution.py:24
  59.7 10.5 %collective-permute-start.7 = (f32[64,1,2048]{2,0,1:T(8,128)S(1)}, f32[64,1,2048]{2,0,1:T(8,128)S(1)}, u32[]{:S(2)}, u32[]{:S(2)}) collective-permute-start(f32[64,1,2048]{2,0,1:T(8,128)S(1)} %get-tuple-element.33), channel_id=1, source_target_pairs={{1,0},{2,1},{3,2},{4,3},{5,4},{6,5},{7,6},{9,8},{10,9},{11,10},{12... | collective-permute-start | bytes 1572872 | tf_op jit(solution)/shard_map/ppermute | solution.py:26
  74.9 8.0 %collective-permute-start.8 = (f32[64,1,2048]{2,0,1:T(8,128)S(1)}, f32[64,1,2048]{2,0,1:T(8,128)S(1)}, u32[]{:S(2)}, u32[]{:S(2)}) collective-permute-start(f32[64,1,2048]{2,0,1:T(8,128)S(1)} %get-tuple-element.28), channel_id=1, source_target_pairs={{0,1},{1,2},{2,3},{3,4},{4,5},{5,6},{6,7},{8,9},{9,10},{10,11},{11... | collective-permute-start | bytes 1572872 | tf_op jit(solution)/shard_map/ppermute | solution.py:24
  76.8 10.5 %collective-permute-start.9 = (f32[64,1,2048]{2,0,1:T(8,128)S(1)}, f32[64,1,2048]{2,0,1:T(8,128)S(1)}, u32[]{:S(2)}, u32[]{:S(2)}) collective-permute-start(f32[64,1,2048]{2,0,1:T(8,128)S(1)} %get-tuple-element.27), channel_id=1, source_target_pairs={{1,0},{2,1},{3,2},{4,3},{5,4},{6,5},{7,6},{9,8},{10,9},{11,10},{12... | collective-permute-start | bytes 1572872 | tf_op jit(solution)/shard_map/ppermute | solution.py:26
  92.0 8.0 %collective-permute-start.10 = (f32[64,1,2048]{2,0,1:T(8,128)S(1)}, f32[64,1,2048]{2,0,1:T(8,128)S(1)}, u32[]{:S(2)}, u32[]{:S(2)}) collective-permute-start(f32[64,1,2048]{2,0,1:T(8,128)S(1)} %get-tuple-element.22), channel_id=1, source_target_pairs={{0,1},{1,2},{2,3},{3,4},{4,5},{5,6},{6,7},{8,9},{9,10},{10,11},{11... | collective-permute-start | bytes 1572872 | tf_op jit(solution)/shard_map/ppermute | solution.py:24
  93.9 10.5 %collective-permute-start.11 = (f32[64,1,2048]{2,0,1:T(8,128)S(1)}, f32[64,1,2048]{2,0,1:T(8,128)S(1)}, u32[]{:S(2)}, u32[]{:S(2)}) collective-permute-start(f32[64,1,2048]{2,0,1:T(8,128)S(1)} %get-tuple-element.21), channel_id=1, source_target_pairs={{1,0},{2,1},{3,2},{4,3},{5,4},{6,5},{7,6},{9,8},{10,9},{11,10},{12... | collective-permute-start | bytes 1572872 | tf_op jit(solution)/shard_map/ppermute | solution.py:26
  109.1 8.0 %collective-permute-start.12 = (f32[64,1,2048]{2,0,1:T(8,128)S(1)}, f32[64,1,2048]{2,0,1:T(8,128)S(1)}, u32[]{:S(2)}, u32[]{:S(2)}) collective-permute-start(f32[64,1,2048]{2,0,1:T(8,128)S(1)} %get-tuple-element.16), channel_id=1, source_target_pairs={{0,1},{1,2},{2,3},{3,4},{4,5},{5,6},{6,7},{8,9},{9,10},{10,11},{11... | collective-permute-start | bytes 1572872 | tf_op jit(solution)/shard_map/ppermute | solution.py:24
  111.0 10.5 %collective-permute-start.13 = (f32[64,1,2048]{2,0,1:T(8,128)S(1)}, f32[64,1,2048]{2,0,1:T(8,128)S(1)}, u32[]{:S(2)}, u32[]{:S(2)}) collective-permute-start(f32[64,1,2048]{2,0,1:T(8,128)S(1)} %get-tuple-element.15), channel_id=1, source_target_pairs={{1,0},{2,1},{3,2},{4,3},{5,4},{6,5},{7,6},{9,8},{10,9},{11,10},{12... | collective-permute-start | bytes 1572872 | tf_op jit(solution)/shard_map/ppermute | solution.py:26
  126.1 16.2 %collective-permute-start.14 = (f32[64,1,2048]{2,0,1:T(8,128)S(1)}, f32[64,1,2048]{2,0,1:T(8,128)S(1)}, u32[]{:S(2)}, u32[]{:S(2)}) collective-permute-start(f32[64,1,2048]{2,0,1:T(8,128)S(1)} %get-tuple-element.10), channel_id=1, source_target_pairs={{0,1},{1,2},{2,3},{3,4},{4,5},{5,6},{6,7},{8,9},{9,10},{10,11},{11... | collective-permute-start | bytes 1572872 | tf_op jit(solution)/shard_map/ppermute | solution.py:24
  128.1 14.3 %collective-permute-start.15 = (f32[64,1,2048]{2,0,1:T(8,128)S(1)}, f32[64,1,2048]{2,0,1:T(8,128)S(1)}, u32[]{:S(2)}, u32[]{:S(2)}) collective-permute-start(f32[64,1,2048]{2,0,1:T(8,128)S(1)} %get-tuple-element.9), channel_id=1, source_target_pairs={{1,0},{2,1},{3,2},{4,3},{5,4},{6,5},{7,6},{9,8},{10,9},{11,10},{12... | collective-permute-start | bytes 1572872 | tf_op jit(solution)/shard_map/ppermute | solution.py:26
  159.5 5.0 %copy-start.3 = (s32[1,4,1024]{2,1,0:T(4,128)S(1)}, s32[1,4,1024]{2,1,0:T(4,128)}, u32[]{:S(2)}) copy-start(s32[1,4,1024]{2,1,0:T(4,128)} %param.8) | copy-start | bytes 49156
  159.5 5.2 %copy-start.4 = (bf16[1,4,1024]{2,1,0:T(4,128)(2,1)S(1)}, bf16[1,4,1024]{2,1,0:T(4,128)(2,1)}, u32[]{:S(2)}) copy-start(bf16[1,4,1024]{2,1,0:T(4,128)(2,1)} %param.9) | copy-start | bytes 24580
  159.5 52.5 %all-to-all-start = ((f32[4,4,64,8,128]{4,3,2,1,0:T(8,128)}), f32[4,4,64,8,128]{4,3,2,1,0:T(8,128)}, u32[]{:S(2)}, u32[]{:S(2)}) async-start(f32[4,4,64,8,128]{4,3,2,1,0:T(8,128)} %bitcast.148), calls=%async_computation | async-start | bytes 8388608 | tf_op jit(solution)/shard_map/all_to_all | solution.py:88
  307.3 19.3 %collective-permute-start.18 = (bf16[4,256]{1,0:T(4,128)(2,1)S(1)}, bf16[4,256]{1,0:T(4,128)(2,1)S(1)}, u32[]{:S(2)}, u32[]{:S(2)}) collective-permute-start(bf16[4,256]{1,0:T(4,128)(2,1)S(1)} %bitcast.153), channel_id=1, source_target_pairs={{0,1},{1,2},{2,3},{3,4},{4,5},{5,6},{6,7},{8,9},{9,10},{10,11},{11... | collective-permute-start | bytes 6152 | tf_op jit(solution)/shard_map/ppermute | solution.py:36
  313.0 13.7 %collective-permute-start.19 = (bf16[4,256]{1,0:T(4,128)(2,1)S(1)}, bf16[4,256]{1,0:T(4,128)(2,1)S(1)}, u32[]{:S(2)}, u32[]{:S(2)}) collective-permute-start(bf16[4,256]{1,0:T(4,128)(2,1)S(1)} %bitcast.154), channel_id=1, source_target_pairs={{1,0},{2,1},{3,2},{4,3},{5,4},{6,5},{7,6},{9,8},{10,9},{11,10},{12... | collective-permute-start | bytes 6152 | tf_op jit(solution)/shard_map/ppermute | solution.py:36
  317.4 9.8 %collective-permute-start.16 = (bf16[4,256,256]{2,1,0:T(8,128)(2,1)S(1)}, bf16[4,256,256]{2,1,0:T(8,128)(2,1)S(1)}, u32[]{:S(2)}, u32[]{:S(2)}) collective-permute-start(bf16[4,256,256]{2,1,0:T(8,128)(2,1)S(1)} %fusion.25), channel_id=1, source_target_pairs={{0,1},{1,2},{2,3},{3,4},{4,5},{5,6},{6,7},{8,9},{9,10},{10,11},{11... | collective-permute-start | bytes 1572872 | tf_op jit(solution)/shard_map/ppermute | solution.py:36
  321.8 10.5 %collective-permute-start.17 = (bf16[4,256,256]{2,1,0:T(8,128)(2,1)S(1)}, bf16[4,256,256]{2,1,0:T(8,128)(2,1)S(1)}, u32[]{:S(2)}, u32[]{:S(2)}) collective-permute-start(bf16[4,256,256]{2,1,0:T(8,128)(2,1)S(1)} %fusion.28), channel_id=1, source_target_pairs={{1,0},{2,1},{3,2},{4,3},{5,4},{6,5},{7,6},{9,8},{10,9},{11,10},{12... | collective-permute-start | bytes 1572872 | tf_op jit(solution)/shard_map/ppermute | solution.py:36
  (3 other events, 10.8 us)
where the time goes:
time: 422 us; the launch traced here: 414 us
  local copies, waits for them, and re-layouts  127 us (30%)
  waiting for transfers between devices  97.5 us (23%)
  starting transfers between devices  63.2 us (15%)
  blocking collectives  49.8 us (12%)
  other arithmetic  41.5 us (10%)
  matrix products  34.3 us (8%)
    gather x2, local copies, waits for them, and re-layouts, local(): picked = jnp.take_along_axis(states, cell_index[:, None, :], axis=2)  74.5 us
    all_to_all x1, blocking collectives, local(): lax.all_to_all(outgoing, 'member', split_axis=2, concat_axis=0, tiled=True)  49.8 us
    all_to_all x1, waiting for transfers between devices, local(): lax.all_to_all(split_state, 'member', split_axis=0, concat_axis=2, tiled=...  47.3 us
    add x8, other arithmetic, advance(): current + step_size * (laplace - advect - damping * current + forcing_rows)  35.3 us
    ppermute x8, waiting for transfers between devices, padded(): lax.ppermute(head, axis, [((i + 1) % count, i) for i in range(ends)])  30.8 us
    ppermute x8, starting transfers between devices, padded(): lax.ppermute(head, axis, [((i + 1) % count, i) for i in range(ends)])  29.1 us
    ppermute x8, starting transfers between devices, padded(): lax.ppermute(tail, axis, [(i, (i + 1) % count) for i in range(ends)])  17.2 us
    slice x16, local copies, waits for them, and re-layouts, advance(): right_cells = jnp.roll(current, -1, axis=2)  15 us
  transfers between devices with their start and end apart: 21, of which 17 were waited for; matrix products, arithmetic and copies ran while one was open for 5% of the time, Pallas kernels for 0%

commit v1 on v0

v1 whole, which is shorter than its diff:
```python
import functools
import math

import jax
import jax.numpy as jnp
from jax import lax
from jax.experimental import pallas as pl
from jax.experimental.pallas import tpu as pltpu
from jax.sharding import PartitionSpec as P

STEPS = 8
ITERS = 6
REGION_COLS = 128
MESH = pl.DeviceIdType.MESH
F32 = jnp.float32
BF16 = jnp.bfloat16
NN = (((1,), (0,)), ((), ()))
NT = (((1,), (1,)), ((), ()))


def dot(a, b, dims=NN):
    return lax.dot_general(a, b, dims, preferred_element_type=F32)


def split(value, pieces):
    out = []
    for _ in range(pieces):
        part = value.astype(BF16)
        out.append(part)
        value = value - part.astype(F32)
    return out


def product(a, b):
    (ah, al), (bh, bl) = a, b
    return dot(
        jnp.concatenate([ah, ah, al], axis=1), jnp.concatenate([bh, bl, bh], axis=0)
    )


def stacked(rows, height, width):
    place = lax.broadcasted_iota(jnp.int32, (height, width), 0)
    out = jnp.zeros((height, width), F32)
    for i, row in enumerate(rows):
        out = jnp.where(place == i, jnp.broadcast_to(row, (height, width)), out)
    return out


def cycle(
    x_ref, drive_ref, y_ref, idx_ref, w_ref,
    dev_out, mean_out,
    state, drive, halo, edge, sums_s, centre_s, send_dev, a_hi, scaled, own_mat, own_vec, near_out, near_in,
    y_hi, y_lo, z_hi, z_lo, ret_dev, ret_mean,
    load_sem, halo_send, halo_recv, fwd_send, fwd_recv, sums_send, sums_recv,
    near_send, near_recv, ret_send, ret_recv, retm_send, retm_recv, keep_sem,
):
    groups = lax.axis_size("member")
    blocks = lax.axis_size("space")
    me = lax.axis_index("member")
    here = lax.axis_index("space")
    _, height, members, cols = state.shape
    regions = idx_ref.shape[0]
    half = members // 2
    everyone = members * groups
    has_above = here > 0
    has_below = here < blocks - 1

    load = pltpu.make_async_copy(x_ref, state.at[0], load_sem)
    load.start()

    barrier = pltpu.get_barrier_semaphore()

    @pl.when(has_above)
    def _():
        pl.semaphore_signal(barrier, inc=1, device_id={"space": here - 1}, device_id_type=MESH)

    @pl.when(has_below)
    def _():
        pl.semaphore_signal(barrier, inc=1, device_id={"space": here + 1}, device_id_type=MESH)

    for k in range(1, groups):
        pl.semaphore_signal(
            barrier, inc=1, device_id={"member": lax.rem(me + k, groups)}, device_id_type=MESH
        )

    for r in range(height):
        drive[r] = jnp.broadcast_to(2.0 * drive_ref[r : r + 1, :], (16, cols))

    @pl.when(jnp.logical_not(has_above))
    def _():
        halo[:, 0] = jnp.zeros(halo[:, 0].shape, BF16)

    @pl.when(jnp.logical_not(has_below))
    def _():
        halo[:, 1] = jnp.zeros(halo[:, 1].shape, BF16)

    sides_here = has_above.astype(jnp.int32) + has_below.astype(jnp.int32)
    pl.semaphore_wait(barrier, groups - 1 + sides_here)
    load.wait()

    def halo_copy(s, d, h):
        target = here + 1 if d == 0 else here - 1
        return pltpu.make_async_remote_copy(
            src_ref=edge.at[s, d, h],
            dst_ref=halo.at[s, d, h],
            send_sem=halo_send.at[s, d, h],
            recv_sem=halo_recv.at[s, d, h],
            device_id={"space": target},
            device_id_type=MESH,
        )

    def send_edges(s, slot, h):
        for d, row, wanted in ((0, height - 1, has_below), (1, 0, has_above)):
            edge[s, d, h] = state[slot, row, h * half : (h + 1) * half, :].astype(BF16)

            @pl.when(wanted)
            def _():
                halo_copy(s, d, h).start()

    def updated(x, north, south, push):
        east = pltpu.roll(x, cols - 1, 1)
        west = pltpu.roll(x, 1, 1)
        return 0.05 * (
            x * (1.0 + ((west - east) + (north - south)))
            + ((east + west) + (8.0 * (north + south) + push))
        )

    def step(s, carry):
        now = lax.rem(s, 2)
        later = 1 - now
        for h in range(2):
            @pl.when(has_above)
            def _():
                halo_copy(s, 0, h).wait_recv()

            @pl.when(has_below)
            def _():
                halo_copy(s, 1, h).wait_recv()

            def edges(t, carry):
                at = pl.multiple_of(t * 16, 16)
                m = pl.ds(pl.multiple_of(h * half + t * 16, 16), 16)
                x = state[now, 0, m, :]
                north = halo[s, 0, h, pl.ds(at, 16), :].astype(F32)
                state[later, 0, m, :] = updated(x, north, state[now, 1, m, :], drive[0])
                x = state[now, height - 1, m, :]
                south = halo[s, 1, h, pl.ds(at, 16), :].astype(F32)
                state[later, height - 1, m, :] = updated(
                    x, state[now, height - 2, m, :], south, drive[height - 1]
                )
                return carry

            lax.fori_loop(0, half // 16, edges, 0)

            @pl.when(s + 1 < STEPS)
            def _():
                send_edges(s + 1, later, h)

            def inner(i, carry):
                r = 1 + i // (half // 16)
                t = i % (half // 16)
                m = pl.ds(pl.multiple_of(h * half + t * 16, 16), 16)
                state[later, r, m, :] = updated(
                    state[now, r, m, :], state[now, r - 1, m, :], state[now, r + 1, m, :], drive[r]
                )
                return carry

            lax.fori_loop(0, (height - 2) * (half // 16), inner, 0)
        return carry

    send_edges(0, 0, 0)
    send_edges(0, 0, 1)
    lax.fori_loop(0, STEPS, step, 0)
    last = STEPS % 2

    def sums_copy(q, p):
        return pltpu.make_async_remote_copy(
            src_ref=sums_s.at[me], dst_ref=sums_s.at[p],
            send_sem=sums_send.at[q], recv_sem=sums_recv.at[p],
            device_id={"member": q}, device_id_type=MESH)

    def add_members(r, carry):
        sums_s[me, pl.ds(r, 1), :] = jnp.sum(state[last, r], axis=0, keepdims=True)
        return carry

    lax.fori_loop(0, height, add_members, 0)
    for k in range(1, groups):
        sums_copy(lax.rem(me + k, groups), me).start()
    for k in range(1, groups):
        peer = lax.rem(me + k, groups)
        sums_copy(peer, peer).wait_recv()
    total = sums_s[0]
    for p in range(1, groups):
        total = total + sums_s[p]
    centre_s[...] = total * (1.0 / everyone)

    def fwd_copy(q, p, g):
        rows = pl.ds(pl.multiple_of(p * members, members), members)
        return pltpu.make_async_remote_copy(
            src_ref=send_dev.at[q, g], dst_ref=a_hi.at[g, rows, :],
            send_sem=fwd_send.at[q, g], recv_sem=fwd_recv.at[p, g],
            device_id={"member": q}, device_id_type=MESH)

    for g in range(regions):
        def pack(q, carry):
            start = pl.multiple_of((q * regions + g) * REGION_COLS, REGION_COLS)
            for r in range(height):
                x = state[last, r, :, pl.ds(start, REGION_COLS)]
                mean = centre_s[r : r + 1, pl.ds(start, REGION_COLS)]
                send_dev[q, g, :, r * REGION_COLS : (r + 1) * REGION_COLS] = (x - mean).astype(BF16)
            return carry

        lax.fori_loop(0, groups, pack, 0)
        for k in range(1, groups):
            fwd_copy(lax.rem(me + k, groups), me, g).start()
        a_hi[g, pl.ds(pl.multiple_of(me * members, members), members), :] = send_dev[me, g]

    row_iota = lax.broadcasted_iota(jnp.int32, (height, REGION_COLS), 0).astype(F32)
    span = float(height)
    from_above = span - row_iota
    from_below = row_iota + 1.0
    taper_down = jnp.exp(-2.0 * from_above * from_above / (span * span))
    taper_up = jnp.exp(-2.0 * from_below * from_below / (span * span))

    def near_copy(g, d):
        target = here + 1 if d == 0 else here - 1
        return pltpu.make_async_remote_copy(
            src_ref=near_out.at[g, d], dst_ref=near_in.at[g, d],
            send_sem=near_send.at[g, d], recv_sem=near_recv.at[g, d],
            device_id={"space": target}, device_id_type=MESH)

    def centre_of(g):
        start = pl.multiple_of((me * regions + g) * REGION_COLS, REGION_COLS)
        return centre_s[:, pl.ds(start, REGION_COLS)]

    def curve(g, carry):
        for k in range(1, groups):
            peer = lax.rem(me + k, groups)
            fwd_copy(peer, peer, g).wait_recv()
        centre = centre_of(g)
        cells = idx_ref[pl.ds(g, 1), :]
        count = cells.shape[1]
        in_row = (
            lax.broadcasted_iota(jnp.int32, (height, count), 0) == cells // REGION_COLS
        ).astype(F32)
        in_col = (
            lax.broadcasted_iota(jnp.int32, (REGION_COLS, count), 0) == cells % REGION_COLS
        ).astype(F32).astype(BF16)
        centre_parts = jnp.concatenate(
            [piece.astype(F32) for piece in split(centre, 3)], axis=0
        ).astype(BF16)
        at_cols = dot(centre_parts, in_col)
        at_cols = at_cols[:height] + at_cols[height : 2 * height] + at_cols[2 * height :]
        obs_mean = jnp.sum(at_cols * in_row, axis=0, keepdims=True)
        innovation = (y_ref[pl.ds(g, 1), :] - obs_mean).astype(BF16).astype(F32)
        weight = w_ref[pl.ds(g, 1), :]
        push_hi, push_lo = split(weight * innovation, 2)
        sums = dot(
            jnp.concatenate(
                [in_row * weight, in_row * push_hi.astype(F32), in_row * push_lo.astype(F32)], axis=0
            ).astype(BF16),
            in_col,
            NT,
        )
        weights = sums[:height]
        pushes = sums[height : 2 * height] + sums[2 * height :]
        weights_down, weights_up = weights * taper_down, weights * taper_up
        pieces = []
        for values in (pushes, pushes * taper_down, pushes * taper_up):
            pieces.extend(piece.astype(F32) for piece in split(values, 3))
        for r in range(height):
            at = slice(r * REGION_COLS, (r + 1) * REGION_COLS)
            a = a_hi[g, :, at].astype(F32)
            for i, values in enumerate((weights, weights_down, weights_up)):
                scaled[i * everyone : (i + 1) * everyone, at] = (a * values[r : r + 1, :]).astype(BF16)
            scaled[3 * everyone :, at] = stacked(
                [piece[r : r + 1, :] for piece in pieces], 16, REGION_COLS
            ).astype(BF16)
        sums_k = dot(scaled[...], a_hi[g], NT)
        vectors = sums_k[3 * everyone :]
        vec = [vectors[3 * i : 3 * i + 1] + vectors[3 * i + 1 : 3 * i + 2] + vectors[3 * i + 2 : 3 * i + 3] for i in range(3)]
        own_mat[g] = sums_k[:everyone]
        own_vec[g] = jnp.broadcast_to(vec[0], (8, everyone))
        for d, wanted in ((0, has_below), (1, has_above)):
            near_out[g, d, :everyone, :] = sums_k[(d + 1) * everyone : (d + 2) * everyone].astype(BF16)
            near_out[g, d, everyone:, :] = stacked(
                [piece.astype(F32) for piece in split(vec[d + 1], 2)], 16, everyone
            ).astype(BF16)

            @pl.when(wanted)
            def _():
                near_copy(g, d).start()
        return carry

    lax.fori_loop(0, regions, curve, 0)

    @pl.when(jnp.logical_not(has_above))
    def _():
        near_in[:, 0] = jnp.zeros(near_in[:, 0].shape, BF16)

    @pl.when(jnp.logical_not(has_below))
    def _():
        near_in[:, 1] = jnp.zeros(near_in[:, 1].shape, BF16)

    def ret_copies(q, g):
        common = dict(device_id={"member": q}, device_id_type=MESH)
        return (
            pltpu.make_async_remote_copy(
                src_ref=ret_dev.at[q, g], dst_ref=dev_out.at[me, g],
                send_sem=ret_send.at[q, g], recv_sem=ret_recv.at[me, g], **common),
            pltpu.make_async_remote_copy(
                src_ref=ret_mean.at[g], dst_ref=mean_out.at[me, g],
                send_sem=retm_send.at[q, g], recv_sem=retm_recv.at[me, g], **common),
        )

    def ret_arrivals(p, g):
        common = dict(device_id={"member": p}, device_id_type=MESH)
        return (
            pltpu.make_async_remote_copy(
                src_ref=ret_dev.at[p, g], dst_ref=dev_out.at[p, g],
                send_sem=ret_send.at[p, g], recv_sem=ret_recv.at[p, g], **common),
            pltpu.make_async_remote_copy(
                src_ref=ret_mean.at[g], dst_ref=mean_out.at[p, g],
                send_sem=retm_send.at[p, g], recv_sem=retm_recv.at[p, g], **common),
        )

    def kept(g):
        return (
            pltpu.make_async_copy(ret_dev.at[me, g], dev_out.at[me, g], keep_sem.at[g, 0]),
            pltpu.make_async_copy(ret_mean.at[g], mean_out.at[me, g], keep_sem.at[g, 1]),
        )

    square = (everyone, everyone)
    eye = (
        lax.broadcasted_iota(jnp.int32, square, 0) == lax.broadcasted_iota(jnp.int32, square, 1)
    )
    pair = 2 if regions % 2 == 0 else 1

    def solve(j, carry):
        def put(hi, lo, l, value):
            hi[l], lo[l] = split(value, 2)

        def middle_of(product_zy):
            return jnp.where(eye, 1.5, 0.0) - 0.5 * product_zy

        sides, norms = [], []
        for l in range(pair):
            g = j * pair + l

            @pl.when(has_above)
            def _():
                near_copy(g, 0).wait_recv()

            @pl.when(has_below)
            def _():
                near_copy(g, 1).wait_recv()

        for l in range(pair):
            g = j * pair + l
            matrix = own_mat[g] + jnp.where(eye, everyone - 1.0, 0.0)
            side = own_vec[g, 0:1, :]
            for d in range(2):
                matrix = matrix + near_in[g, d, :everyone, :].astype(F32)
                tail = near_in[g, d, everyone:, :].astype(F32)
                side = side + tail[0:1] + tail[1:2]
            norm = jnp.sqrt(jnp.sum(matrix * matrix, keepdims=True))
            sides.append(side)
            norms.append(norm)
            iterate = matrix / norm
            middle = middle_of(iterate)
            z = split(middle, 2)
            z_hi[l], z_lo[l] = z
            put(y_hi, y_lo, l, product(split(iterate, 2), z))

        def sweep(i, carry):
            middles = [
                split(middle_of(product((z_hi[l], z_lo[l]), (y_hi[l], y_lo[l]))), 2)
                for l in range(pair)
            ]
            ys = [product((y_hi[l], y_lo[l]), middles[l]) for l in range(pair)]
            zs = [product(middles[l], (z_hi[l], z_lo[l])) for l in range(pair)]
            for l in range(pair):
                put(y_hi, y_lo, l, ys[l])
                put(z_hi, z_lo, l, zs[l])
            return carry

        lax.fori_loop(0, ITERS - 2, sweep, 0)
        middles = [
            split(middle_of(product((z_hi[l], z_lo[l]), (y_hi[l], y_lo[l]))), 2)
            for l in range(pair)
        ]
        inverses = [product(middles[l], (z_hi[l], z_lo[l])) for l in range(pair)]
        for l in range(pair):
            g = j * pair + l
            zt = split(inverses[l].T, 2)

            def apply(row):
                parts = stacked([p.astype(F32) for p in split(row, 3)], 16, everyone).astype(BF16)
                out = dot(parts, zt[0]) + dot(parts, zt[1])
                return out[0:1] + out[1:2] + out[2:3]

            shift = apply(apply(sides[l])) / norms[l]
            parts = stacked([p.astype(F32) for p in split(shift, 3)], 16, everyone).astype(BF16)
            moved = dot(parts, a_hi[g])
            moved = moved[0:1] + moved[1:2] + moved[2:3]
            gain = math.sqrt(everyone - 1.0) / jnp.sqrt(norms[l])
            deviation = gain * (dot(zt[0], a_hi[g]) + dot(zt[1], a_hi[g]))
            centre = centre_of(g)
            for r in range(height):
                at = slice(r * REGION_COLS, (r + 1) * REGION_COLS)
                ret_mean[g, r : r + 1, :] = centre[r : r + 1, :] + moved[:, at]
                for q in range(groups):
                    ret_dev[q, g, r] = deviation[q * members : (q + 1) * members, at].astype(BF16)
            for k in range(1, groups):
                for copy in ret_copies(lax.rem(me + k, groups), g):
                    copy.start()
            for copy in kept(g):
                copy.start()
        return carry

    lax.fori_loop(0, regions // pair, solve, 0)

    def finish(g, carry):
        for copy in kept(g):
            copy.wait()
        for k in range(1, groups):
            peer = lax.rem(me + k, groups)
            for copy in ret_arrivals(peer, g):
                copy.wait_recv()
            for copy in ret_copies(peer, g) + (fwd_copy(peer, me, g),):
                copy.wait_send()
        for d, wanted in ((0, has_below), (1, has_above)):
            @pl.when(wanted)
            def _():
                near_copy(g, d).wait_send()
        return carry

    lax.fori_loop(0, regions, finish, 0)
    for k in range(1, groups):
        sums_copy(lax.rem(me + k, groups), me).wait_send()

    def drain(s, carry):
        for h in range(2):
            for d, wanted in ((0, has_below), (1, has_above)):
                @pl.when(wanted)
                def _():
                    halo_copy(s, d, h).wait_send()
        return carry

    lax.fori_loop(0, STEPS, drain, 0)


def local(prior_samples, external_drive, obs_value, obs_index, obs_weight):
    members, height, cols = prior_samples.shape
    groups = lax.axis_size("member")
    regions, count = obs_index.shape[1:]
    everyone = members * groups
    cells = height * REGION_COLS
    half = members // 2
    vmem = pl.BlockSpec(memory_space=pltpu.VMEM)
    anywhere = pl.BlockSpec(memory_space=pl.ANY)
    dma = pltpu.SemaphoreType.DMA
    dev_shape = (groups, regions, height, members, REGION_COLS)
    mean_shape = (groups, regions, height, REGION_COLS)
    matrices = (2, everyone, everyone)
    dev, mean = pl.pallas_call(
        cycle,
        out_shape=(
            jax.ShapeDtypeStruct(dev_shape, BF16),
            jax.ShapeDtypeStruct(mean_shape, F32),
        ),
        in_specs=[anywhere, vmem, vmem, vmem, vmem],
        out_specs=(anywhere, anywhere),
        scratch_shapes=[
            pltpu.VMEM((2, height, members, cols), F32),
            pltpu.VMEM((height, 16, cols), F32),
            pltpu.VMEM((STEPS, 2, 2, half, cols), BF16),
            pltpu.VMEM((STEPS, 2, 2, half, cols), BF16),
            pltpu.VMEM((groups, height, cols), F32),
            pltpu.VMEM((height, cols), F32),
            pltpu.VMEM((groups, regions, members, cells), BF16),
            pltpu.VMEM((regions, everyone, cells), BF16),
            pltpu.VMEM((3 * everyone + 16, cells), BF16),
            pltpu.VMEM((regions, everyone, everyone), F32),
            pltpu.VMEM((regions, 8, everyone), F32),
            pltpu.VMEM((regions, 2, everyone + 16, everyone), BF16),
            pltpu.VMEM((regions, 2, everyone + 16, everyone), BF16),
            pltpu.VMEM(matrices, BF16),
            pltpu.VMEM(matrices, BF16),
            pltpu.VMEM(matrices, BF16),
            pltpu.VMEM(matrices, BF16),
            pltpu.VMEM(dev_shape, BF16),
            pltpu.VMEM(mean_shape[1:], F32),
            dma,
            dma((STEPS, 2, 2)),
            dma((STEPS, 2, 2)),
            dma((groups, regions)),
            dma((groups, regions)),
            dma((groups,)),
            dma((groups,)),
            dma((regions, 2)),
            dma((regions, 2)),
            dma((groups, regions)),
            dma((groups, regions)),
            dma((groups, regions)),
            dma((groups, regions)),
            dma((regions, 2)),
        ],
        compiler_params=pltpu.CompilerParams(
            collective_id=0, has_side_effects=True, vmem_limit_bytes=56 * 1024 * 1024
        ),
        cost_estimate=pl.CostEstimate(
            flops=20_000_000_000, bytes_accessed=20_000_000, transcendentals=0
        ),
    )(
        prior_samples.transpose(1, 0, 2),
        external_drive,
        obs_value[0],
        obs_index[0],
        obs_weight[0].astype(F32),
    )
    out = dev.astype(F32) + mean[:, :, :, None, :]
    return out.transpose(3, 2, 0, 1, 4).reshape(members, height, cols)


def solution(mesh):
    return jax.shard_map(
        local,
        mesh=mesh,
        in_specs=(
            P("member", "space", None),
            P("space", None),
            P("space", "member", None),
            P("space", "member", None),
            P("space", "member", None),
        ),
        out_specs=P("member", "space", None),
        check_vma=False,
    )
```

time: 422 us -> 126 us (0.30); the launches traced: 414 us -> 126 us
  local copies, waits for them, and re-layouts: 127 us -> 11.1 us
  Pallas kernels: 0 us -> 111 us
  waiting for transfers between devices: 97.5 us -> 0 us
  starting transfers between devices: 63.2 us -> 0 us
  blocking collectives: 49.8 us -> 0 us
  other arithmetic: 41.5 us -> 3.56 us
  matrix products: 34.3 us -> 0 us
    pallas_call x0 -> x1, Pallas kernels: none -> 111 us  [local(): pl.pallas_call(cycle, out_shape=(jax.ShapeDtypeStruct(dev_shape, BF16), j...]
    gather x2 -> x0, local copies, waits for them, and re-layouts: 74.5 us -> none  [local(): picked = jnp.take_along_axis(states, cell_index[:, None, :], axis=2)]
    ppermute x20 -> x0, starting transfers between devices: 58.2 us -> none  [the longest x8 29.1 us: padded(): lax.ppermute(head, axis, [((i + 1) % count, i) for i in range(ends)])]
    ppermute x20 -> x0, waiting for transfers between devices: 50.1 us -> none  [the longest x8 30.8 us: padded(): lax.ppermute(head, axis, [((i + 1) % count, i) for i in range(ends)])]
    all_to_all x1 -> x0, blocking collectives: 49.8 us -> none  [local(): lax.all_to_all(outgoing, 'member', split_axis=2, concat_axis=0, tiled=True)]
    all_to_all x1 -> x0, waiting for transfers between devices: 47.3 us -> none  [local(): lax.all_to_all(split_state, 'member', split_axis=0, concat_axis=2, tiled=...]
    add x9 -> x0, other arithmetic: 35.3 us -> none  [the longest x8 35.3 us: advance(): current + step_size * (laplace - advect - damping * current + forcing_rows)]
    dot_general x26 -> x0, matrix products: 34.3 us -> none  [the longest x6 7.23 us: local(): jnp.einsum('rij,rjk->rik', inverse, iterate, precision=highest)]
  transfers between devices with their start and end apart: 21 -> 0, of which waited for: 17 -> 0; matrix products, arithmetic and copies ran while one was open for 5% -> 0% of each run, Pallas kernels for 0% -> 0%
where the time goes in v1:
time: 126 us
  Pallas kernels  111 us (88%)
  local copies, waits for them, and re-layouts  11.1 us (9%)
  other arithmetic  3.56 us (3%)
    pallas_call x1, Pallas kernels, local(): pl.pallas_call(cycle, out_shape=(jax.ShapeDtypeStruct(dev_shape, BF16), j...  111 us
    unnamed x1, local copies, waits for them, and re-layouts  6.63 us
    transpose x1, local copies, waits for them, and re-layouts, local(): return out.transpose(3, 2, 0, 1, 4).reshape(members, height, cols)  4.44 us

profile of v1, /device:TPU:9, one launch (start us, length us, event | category | flops | bytes accessed | tf_op | source)
XLA Modules:
  0.0 125.7 jit_solution(9864899215500849853)
XLA Ops:
  0.0 1.3 %bitcast_convert_fusion.w_ref = f32[4,1024]{1,0:T(4,128)} fusion(bf16[1,4,1024]{2,1,0:T(4,128)(2,1)} %param.9), kind=kLoop, calls=%fused_computation.2 | loop fusion | flops 4096 | bytes 24576 | tf_op jit(solution)/shard_map/convert_element_type | solution.py:520
  1.3 6.6 %copy.10 = f32[64,8,2048]{2,0,1:T(8,128)} copy(f32[64,8,2048]{2,1,0:T(8,128)} %param.5) | data formatting | bytes 8388608 | tf_op args[0]
  7.9 111.0 %shard_map.55 = (bf16[4,4,8,64,128]{4,3,2,1,0:T(8,128)(2,1)}, f32[4,4,8,128]{3,2,1,0:T(8,128)}) custom-call(f32[8,64,2048]{2,1,0:T(8,128)} %bitcast.11, f32[8,2048]{1,0:T(8,128)} %drive_ref.1, f32[4,1024]{1,0:T(4,128)} %bitcast.12, s32[4,1024]{1,0:T(4,128)} %bitcast.13, f32[4,1024]{1,0:T(4,128)} %bitcast_convert_fusion.w_ref), custom_call_target="tpu_custom_call" | custom-call | flops 20000000000 | bytes 20000000 | tf_op jit(solution)/shard_map/pallas_call | solution.py:466
  118.9 2.3 %add_bitcast_fusion = f32[64,8,4,4,128]{4,0,1,3,2:T(8,128)S(1)} fusion(bf16[4,4,8,64,128]{4,3,2,1,0:T(8,128)(2,1)} %get-tuple-element.7, f32[4,4,8,128]{3,2,1,0:T(8,128)} %get-tuple-element.8), kind=kLoop, calls=%fused_computation.1 | loop fusion | flops 2097152 | bytes 6356992 | tf_op jit(solution)/shard_map/transpose | solution.py:523
  121.2 4.4 %copy.8 = f32[64,8,4,4,128]{4,1,3,2,0:T(8,128)} copy(f32[64,8,4,4,128]{4,0,1,3,2:T(8,128)S(1)} %add_bitcast_fusion) | data formatting | bytes 8388608 | tf_op jit(solution)/shard_map/transpose | solution.py:523

commit v2 on v1

--- a/solution.py
+++ b/solution.py
@@ -49,7 +49,7 @@
 def cycle(
     x_ref, drive_ref, y_ref, idx_ref, w_ref,
     dev_out, mean_out,
-    state, drive, halo, edge, sums_s, centre_s, send_dev, a_hi, scaled, own_mat, own_vec, near_out, near_in,
+    x_buf, w_s, state, drive, halo, edge, sums_s, centre_s, send_dev, a_hi, scaled, own_mat, own_vec, near_out, near_in,
     y_hi, y_lo, z_hi, z_lo, ret_dev, ret_mean,
     load_sem, halo_send, halo_recv, fwd_send, fwd_recv, sums_send, sums_recv,
     near_send, near_recv, ret_send, ret_recv, retm_send, retm_recv, keep_sem,
@@ -65,8 +65,20 @@
     has_above = here > 0
     has_below = here < blocks - 1
 
-    load = pltpu.make_async_copy(x_ref, state.at[0], load_sem)
-    load.start()
+    cut = half * height
+    tiles = cols // REGION_COLS
+
+    def load(h, c):
+        rows = slice(h * cut, (h + 1) * cut)
+        at = pl.ds(pl.multiple_of(c * REGION_COLS, REGION_COLS), REGION_COLS)
+        return pltpu.make_async_copy(x_ref.at[rows, at], x_buf.at[c, rows], load_sem.at[h, c])
+
+    for h in range(2):
+        def begin(c, carry):
+            load(h, c).start()
+            return carry
+
+        lax.fori_loop(0, tiles, begin, 0)
 
     barrier = pltpu.get_barrier_semaphore()
 
@@ -94,9 +106,9 @@
     def _():
         halo[:, 1] = jnp.zeros(halo[:, 1].shape, BF16)
 
+    w_s[...] = w_ref[0].astype(F32)
     sides_here = has_above.astype(jnp.int32) + has_below.astype(jnp.int32)
     pl.semaphore_wait(barrier, groups - 1 + sides_here)
-    load.wait()
 
     def halo_copy(s, d, h):
         target = here + 1 if d == 0 else here - 1
@@ -168,8 +180,24 @@
             lax.fori_loop(0, (height - 2) * (half // 16), inner, 0)
         return carry
 
-    send_edges(0, 0, 0)
-    send_edges(0, 0, 1)
+    def unfold(h, rows, wait):
+        def tile(c, carry):
+            if wait:
+                load(h, c).wait()
+            at = pl.ds(pl.multiple_of(c * REGION_COLS, REGION_COLS), REGION_COLS)
+            for r in rows:
+                state[0, r, h * half : (h + 1) * half, at] = x_buf[
+                    c, pl.ds(h * cut + r, half, stride=height), :
+                ]
+            return carry
+
+        lax.fori_loop(0, tiles, tile, 0)
+
+    for h in range(2):
+        unfold(h, (0, height - 1), True)
+        send_edges(0, 0, h)
+    for h in range(2):
+        unfold(h, range(1, height - 1), False)
     lax.fori_loop(0, STEPS, step, 0)
     last = STEPS % 2
 
@@ -234,9 +262,6 @@
         return centre_s[:, pl.ds(start, REGION_COLS)]
 
     def curve(g, carry):
-        for k in range(1, groups):
-            peer = lax.rem(me + k, groups)
-            fwd_copy(peer, peer, g).wait_recv()
         centre = centre_of(g)
         cells = idx_ref[pl.ds(g, 1), :]
         count = cells.shape[1]
@@ -253,7 +278,7 @@
         at_cols = at_cols[:height] + at_cols[height : 2 * height] + at_cols[2 * height :]
         obs_mean = jnp.sum(at_cols * in_row, axis=0, keepdims=True)
         innovation = (y_ref[pl.ds(g, 1), :] - obs_mean).astype(BF16).astype(F32)
-        weight = w_ref[pl.ds(g, 1), :]
+        weight = w_s[pl.ds(g, 1), :]
         push_hi, push_lo = split(weight * innovation, 2)
         sums = dot(
             jnp.concatenate(
@@ -268,6 +293,9 @@
         pieces = []
         for values in (pushes, pushes * taper_down, pushes * taper_up):
             pieces.extend(piece.astype(F32) for piece in split(values, 3))
+        for k in range(1, groups):
+            peer = lax.rem(me + k, groups)
+            fwd_copy(peer, peer, g).wait_recv()
         for r in range(height):
             at = slice(r * REGION_COLS, (r + 1) * REGION_COLS)
             a = a_hi[g, :, at].astype(F32)
@@ -292,8 +320,6 @@
                 near_copy(g, d).start()
         return carry
 
-    lax.fori_loop(0, regions, curve, 0)
-
     @pl.when(jnp.logical_not(has_above))
     def _():
         near_in[:, 0] = jnp.zeros(near_in[:, 0].shape, BF16)
@@ -334,7 +360,7 @@
     eye = (
         lax.broadcasted_iota(jnp.int32, square, 0) == lax.broadcasted_iota(jnp.int32, square, 1)
     )
-    pair = 2 if regions % 2 == 0 else 1
+    pair = 1
 
     def solve(j, carry):
         def put(hi, lo, l, value):
@@ -366,7 +392,7 @@
             norm = jnp.sqrt(jnp.sum(matrix * matrix, keepdims=True))
             sides.append(side)
             norms.append(norm)
-            iterate = matrix / norm
+            iterate = matrix * (1.0 / norm)
             middle = middle_of(iterate)
             z = split(middle, 2)
             z_hi[l], z_lo[l] = z
@@ -418,7 +444,18 @@
                 copy.start()
         return carry
 
-    lax.fori_loop(0, regions // pair, solve, 0)
+    def advance(g, carry):
+        @pl.when(g < regions)
+        def _():
+            curve(g, 0)
+
+        @pl.when(g > 0)
+        def _():
+            solve(g - 1, 0)
+
+        return carry
+
+    lax.fori_loop(0, regions + 1, advance, 0)
 
     def finish(g, carry):
         for copy in kept(g):
@@ -448,6 +485,29 @@
         return carry
 
     lax.fori_loop(0, STEPS, drain, 0)
+
+
+def assemble(dev_ref, mean_ref, out_ref, folded, sem):
+    _, regions, height, members, _ = dev_ref.shape
+    p = pl.program_id(0)
+    tiles = folded.shape[0]
+
+    def store(c):
+        at = pl.ds(pl.multiple_of(c * REGION_COLS, REGION_COLS), REGION_COLS)
+        return pltpu.make_async_copy(folded.at[c], out_ref.at[:, at], sem.at[c])
+
+    for g in range(regions):
+        c = p * regions + g
+        for r in range(height):
+            folded[c, pl.ds(r, members, stride=height), :] = (
+                dev_ref[0, g, r].astype(F32) + mean_ref[0, g, r : r + 1, :]
+            )
+        store(c).start()
+
+    @pl.when(p == pl.num_programs(0) - 1)
+    def _():
+        for c in range(tiles):
+            store(c).wait()
 
 
 def local(prior_samples, external_drive, obs_value, obs_index, obs_weight):
@@ -462,7 +522,7 @@
     dma = pltpu.SemaphoreType.DMA
     dev_shape = (groups, regions, height, members, REGION_COLS)
     mean_shape = (groups, regions, height, REGION_COLS)
-    matrices = (2, everyone, everyone)
+    matrices = (1, everyone, everyone)
     dev, mean = pl.pallas_call(
         cycle,
         out_shape=(
@@ -472,6 +532,8 @@
         in_specs=[anywhere, vmem, vmem, vmem, vmem],
         out_specs=(anywhere, anywhere),
         scratch_shapes=[
+            pltpu.VMEM((cols // REGION_COLS, members * height, REGION_COLS), F32),
+            pltpu.VMEM((regions, count), F32),
             pltpu.VMEM((2, height, members, cols), F32),
             pltpu.VMEM((height, 16, cols), F32),
             pltpu.VMEM((STEPS, 2, 2, half, cols), BF16),
@@ -491,7 +553,7 @@
             pltpu.VMEM(matrices, BF16),
             pltpu.VMEM(dev_shape, BF16),
             pltpu.VMEM(mean_shape[1:], F32),
-            dma,
+            dma((2, cols // REGION_COLS)),
             dma((STEPS, 2, 2)),
             dma((STEPS, 2, 2)),
             dma((groups, regions)),
@@ -513,14 +575,29 @@
             flops=20_000_000_000, bytes_accessed=20_000_000, transcendentals=0
         ),
     )(
-        prior_samples.transpose(1, 0, 2),
+        prior_samples.reshape(members * height, cols),
         external_drive,
         obs_value[0],
         obs_index[0],
-        obs_weight[0].astype(F32),
+        obs_weight,
     )
-    out = dev.astype(F32) + mean[:, :, :, None, :]
-    return out.transpose(3, 2, 0, 1, 4).reshape(members, height, cols)
+    out = pl.pallas_call(
+        assemble,
+        grid=(groups,),
+        out_shape=jax.ShapeDtypeStruct((members * height, cols), F32),
+        in_specs=[
+            pl.BlockSpec((1,) + dev_shape[1:], lambda p: (p, 0, 0, 0, 0)),
+            pl.BlockSpec((1,) + mean_shape[1:], lambda p: (p, 0, 0, 0)),
+        ],
+        out_specs=anywhere,
+        scratch_shapes=[
+            pltpu.VMEM((cols // REGION_COLS, members * height, REGION_COLS), F32),
+            dma((cols // REGION_COLS,)),
+        ],
+        compiler_params=pltpu.CompilerParams(vmem_limit_bytes=24 * 1024 * 1024),
+        cost_estimate=pl.CostEstimate(flops=2_000_000, bytes_accessed=7_000_000, transcendentals=0),
+    )(dev, mean)
+    return out.reshape(members, height, cols)
 
 
 def solution(mesh):

time: 126 us -> 107 us (0.85)
  local copies, waits for them, and re-layouts: 11.1 us -> 2.42 us
  Pallas kernels: 111 us -> 104 us
  other arithmetic: 3.56 us -> 0 us
    pallas_call x1, Pallas kernels: 111 us -> 102 us  [local(): pl.pallas_call(cycle, out_shape=(jax.ShapeDtypeStruct(dev_shape, BF16), j...]
    transpose x1 -> x0, local copies, waits for them, and re-layouts: 4.44 us -> none  [local(): return out.transpose(3, 2, 0, 1, 4).reshape(members, height, cols)]
    unnamed x1 -> x4, local copies, waits for them, and re-layouts: 6.63 us -> 2.42 us
    transpose x1 -> x0, other arithmetic: 2.26 us -> none  [local(): return out.transpose(3, 2, 0, 1, 4).reshape(members, height, cols)]
    pallas_call x0 -> x1, Pallas kernels: none -> 2.19 us  [local(): pl.pallas_call(assemble, grid=(groups,), out_shape=jax.ShapeDtypeStruct((...]
    convert_element_type x1 -> x0, other arithmetic: 1.3 us -> none  [local(): obs_weight[0].astype(F32)]
where the time goes in v2:
time: 107 us
  Pallas kernels  104 us (97%)
  local copies, waits for them, and re-layouts  2.42 us (2%)
    pallas_call x1, Pallas kernels, local(): pl.pallas_call(cycle, out_shape=(jax.ShapeDtypeStruct(dev_shape, BF16), j...  102 us
    unnamed x4, local copies, waits for them, and re-layouts  2.42 us
    pallas_call x1, Pallas kernels, local(): pl.pallas_call(assemble, grid=(groups,), out_shape=jax.ShapeDtypeStruct((...  2.19 us

profile of v2, /device:TPU:9, one launch (start us, length us, event | category | flops | bytes accessed | tf_op | source)
XLA Modules:
  0.0 106.9 jit_solution(18332325684022358110)
XLA Ops:
  0.0 102.2 %shard_map.55 = (bf16[4,4,8,64,128]{4,3,2,1,0:T(8,128)(2,1)}, f32[4,4,8,128]{3,2,1,0:T(8,128)}) custom-call(f32[512,2048]{1,0:T(8,128)} %bitcast.4, f32[8,2048]{1,0:T(8,128)} %drive_ref.1, f32[4,1024]{1,0:T(4,128)} %bitcast.5, s32[4,1024]{1,0:T(4,128)} %bitcast.6, bf16[1,4,1024]{2,1,0:T(4,128)(2,1)} %w_ref.1), custom_call_target="tpu_custom_call" | custom-call | flops 20000000000 | bytes 20000000 | tf_op jit(solution)/shard_map/pallas_call | solution.py:526
  102.3 0.0 copy-start
  102.3 1.6 %copy-done = bf16[4,4,8,64,128]{4,3,2,1,0:T(8,128)(2,1)S(1)} copy-done((bf16[4,4,8,64,128]{4,3,2,1,0:T(8,128)(2,1)S(1)}, bf16[4,4,8,64,128]{4,3,2,1,0:T(8,128)(2,1)}, u32[]{:S(2)}) %copy-start) | copy-done | bytes 2097176
  103.8 0.0 copy-start.1
  103.8 0.8 copy-done.1
  104.7 2.2 %shard_map.56 = f32[512,2048]{1,0:T(8,128)} custom-call(bf16[4,4,8,64,128]{4,3,2,1,0:T(8,128)(2,1)S(1)} %copy-done, f32[4,4,8,128]{3,2,1,0:T(8,128)S(1)} %copy-done.1), custom_call_target="tpu_custom_call" | custom-call | flops 2000000 | bytes 7000000 | tf_op jit(solution)/shard_map/pallas_call | solution.py:584
Async XLA Ops:
  102.3 1.6 %copy-start = (bf16[4,4,8,64,128]{4,3,2,1,0:T(8,128)(2,1)S(1)}, bf16[4,4,8,64,128]{4,3,2,1,0:T(8,128)(2,1)}, u32[]{:S(2)}) copy-start(bf16[4,4,8,64,128]{4,3,2,1,0:T(8,128)(2,1)} %get-tuple-element.7.dev_ref) | copy-start | bytes 6291460
  103.8 0.8 copy-start.1
